TPU v7x, 256 devices: a whole 4x4x8 slice. The times are simulated.
256 devices in a mesh: atm: 32 (over x, z), ocn: 8 (over y, core).
Axes of the slice: x: 4, y: 4, z: 8, core: 2. Of those that a mesh axis runs over, the one named last changes fastest.
Arguments:
- state: bfloat16 [1048576, 256], P(('atm', 'ocn')), may hold values from -6 to 6
- branch_id: int32 [1048576], P(('atm', 'ocn')), may hold values from 0 to 1, as said below
- span_map: int32 [65536], P(('atm', 'ocn')), may hold values from 0 to 65535, as said below
- derivative: bfloat16 [16, 16], replicated, may hold values from -1.5 to 1.5
- rad_weight: bfloat16 [256, 2048], replicated, may hold values from -0.375 to 0.375
- conv_in: bfloat16 [256, 2048], replicated, may hold values from -0.375 to 0.375
- conv_out: bfloat16 [2048, 256], replicated, may hold values from -0.125 to 0.125
- flux_weight: bfloat16 [256, 4], replicated, may hold values from -0.375 to 0.375
- remap_cell: int32 [4, 1048576], P(None, ('atm', 'ocn')), may hold values from 0 to 4095
- remap_weight: float32 [4, 1048576], P(None, ('atm', 'ocn')), may hold values from 0.02 to 0.25
- ocean_state: float32 [2, 131072], P(None, ('atm', 'ocn')), may hold values from -6 to 6
- ocean_mask: int32 [131072], P(('atm', 'ocn')), may hold values 0 or 1
- couple: float32 [4, 2], replicated, may hold values from -3 to 3
Outputs:
- new_state: bfloat16 [1048576, 256], P(('atm', 'ocn'))
- span_tend: bfloat16 [1048576, 256], P(('atm', 'ocn'))
- ocean_new: float32 [2, 131072], P(None, ('atm', 'ocn'))
- surface: float32 [2, 1048576], P(None, ('atm', 'ocn'))
Inputs may be any that keep to these rules, and one draw needn't show every extreme that they name: span_map is a permutation of the elements; the place span_map gives an element (a block of 16 rows in span layout) lies on a device with the same ocn index; each device keeps 256 // 2 of its elements on itself and sends exactly 8 to each of 16 other devices with its ocn index, none to the rest. `branch_id`: every physics span (the 256 elements that span_map places on one device) holds exactly 1024 columns with id 1. `remap_cell`: an index into the 4096 ocean cells of the devices with the column's atm index.
All inputs are finite; a program needn't handle non-finite values. No bound on the sum of `ocean_mask` on one device may be relied on, other than what follows from the above.
Results may differ from a plain program's by a relative error of at most 0.012.
Values may be sent and summed in bfloat16 or wider, within the bound.
A program may use at most 64 MiB of HBM per device.

v0:
```python
import jax
import jax.numpy as jnp
from jax import lax
from jax.sharding import PartitionSpec as P


def radiation(x, rad_weight):
    row_count, feat_count = x.shape
    band_count = rad_weight.shape[1] // feat_count
    block_rows = min(512, row_count)

    def radiation_one_block(rows_in):
        band_terms = jnp.dot(rows_in, rad_weight, preferred_element_type=jnp.float32)
        return 0.25 * jnp.sum(
            jnp.tanh(band_terms.reshape(block_rows, band_count, feat_count)), axis=1
        )

    result = lax.map(
        radiation_one_block, x.reshape(row_count // block_rows, block_rows, feat_count)
    )
    return result.reshape(row_count, feat_count)


def convection(x, conv_in, conv_out):
    row_count, feat_count = x.shape
    block_rows = min(512, row_count)

    def convection_one_block(rows_in):
        hidden = jax.nn.silu(jnp.dot(rows_in, conv_in, preferred_element_type=jnp.float32)).astype(
            jnp.bfloat16
        )
        return jnp.dot(hidden, conv_out, preferred_element_type=jnp.float32)

    result = lax.map(
        convection_one_block, x.reshape(row_count // block_rows, block_rows, feat_count)
    )
    return result.reshape(row_count, feat_count)


def body(
    state,
    branch_id,
    span_map,
    derivative,
    rad_weight,
    conv_in,
    conv_out,
    flux_weight,
    remap_cell,
    remap_weight,
    ocean_state,
    ocean_mask,
    couple,
):
    col_count, feat_count = state.shape
    node_count = derivative.shape[0]
    elem_count = col_count // node_count
    peer_count = lax.axis_size("atm")
    ocn_count = lax.axis_size("ocn")
    my_index = lax.axis_index("atm")
    per_peer = elem_count // peer_count
    nsrf_count = ocean_state.shape[0]
    mask_f = ocean_mask.astype(jnp.float32)
    elements = state.reshape(elem_count, node_count, feat_count)
    dynamics = jnp.einsum(
        "ij,ejf->eif", derivative, elements, preferred_element_type=jnp.float32
    ).reshape(col_count, feat_count)
    target = span_map // elem_count // ocn_count
    dest_slot = span_map % elem_count
    stays_home = target == my_index
    onehot = (target[:, None] == jnp.arange(peer_count, dtype=jnp.int32)[None, :]).astype(jnp.int32)
    peer_rank = jnp.sum((jnp.cumsum(onehot, axis=0) - onehot) * onehot, axis=1)
    buffer_pos = jnp.where(stays_home, peer_count * per_peer, target * per_peer + peer_rank)
    source = (
        jnp.full((peer_count * per_peer,), elem_count, jnp.int32)
        .at[buffer_pos]
        .set(jnp.arange(elem_count, dtype=jnp.int32), mode="drop")
    )
    zero_elem = jnp.zeros((1, node_count, feat_count), jnp.bfloat16)
    padded_slot = jnp.concatenate([dest_slot, jnp.full((1,), elem_count, jnp.int32)])
    send_slot = padded_slot[source].reshape(peer_count, per_peer)
    home_slot = jnp.where(stays_home, dest_slot, elem_count)
    safe_pos = jnp.clip(buffer_pos, 0, peer_count * per_peer - 1)
    padded_branch = jnp.concatenate(
        [branch_id.reshape(elem_count, node_count), jnp.zeros((1, node_count), jnp.int32)]
    )
    send_branch = padded_branch[source].reshape(peer_count, per_peer * node_count)
    send_cols = jnp.concatenate([elements, zero_elem])[source].reshape(
        peer_count, per_peer * node_count, feat_count
    )
    recv_slot, recv_branch = (
        lax.all_to_all(send_slot, "atm", split_axis=0, concat_axis=0, tiled=True),
        lax.all_to_all(send_branch, "atm", split_axis=0, concat_axis=0, tiled=True),
    )
    recv_cols = lax.all_to_all(send_cols, "atm", split_axis=0, concat_axis=0, tiled=True)
    all_slot = jnp.concatenate([home_slot, recv_slot.reshape(-1)])
    span_cols = (
        jnp.zeros((elem_count, node_count, feat_count), jnp.bfloat16)
        .at[all_slot]
        .set(
            jnp.concatenate([elements, recv_cols.reshape(-1, node_count, feat_count)]), mode="drop"
        )
    )
    span_branch = (
        jnp.zeros((elem_count, node_count), jnp.int32)
        .at[all_slot]
        .set(
            jnp.concatenate(
                [branch_id.reshape(elem_count, node_count), recv_branch.reshape(-1, node_count)]
            ),
            mode="drop",
        )
    )
    span_rows = span_cols.reshape(col_count, feat_count)
    conv_rows = jnp.nonzero(span_branch.reshape(col_count) == 1, size=col_count // 4)[0].astype(
        jnp.int32
    )
    radiative = radiation(span_rows, rad_weight)
    convective = convection(span_rows[conv_rows], conv_in, conv_out)
    span_tend = radiative.at[conv_rows].add(convective).astype(jnp.bfloat16)
    padded_tend = jnp.concatenate(
        [span_tend.reshape(elem_count, node_count, feat_count), zero_elem]
    )
    send_back = padded_tend[recv_slot.reshape(-1)].reshape(
        peer_count, per_peer * node_count, feat_count
    )
    returned = lax.all_to_all(send_back, "atm", split_axis=0, concat_axis=0, tiled=True).reshape(
        peer_count * per_peer, node_count, feat_count
    )
    own_tend = jnp.where(
        stays_home[:, None, None],
        padded_tend[jnp.minimum(dest_slot, elem_count)],
        returned[safe_pos],
    )
    tendency = own_tend.reshape(col_count, feat_count)
    new_state = (state.astype(jnp.float32) + dynamics + tendency.astype(jnp.float32)).astype(
        jnp.bfloat16
    )
    surface_flux = jnp.dot(tendency, flux_weight, preferred_element_type=jnp.float32)
    nflx_count = surface_flux.shape[1]
    oc_dev = ocean_state.shape[1]
    oc_grp = oc_dev * ocn_count
    weighted = (remap_weight[:, :, None] * surface_flux[None, :, :]).reshape(-1, nflx_count)
    flux_term = jax.ops.segment_sum(weighted, remap_cell.reshape(-1), num_segments=oc_grp).T
    flux_share = lax.psum_scatter(
        flux_term.astype(jnp.bfloat16), "ocn", scatter_dimension=1, tiled=True
    ).astype(jnp.float32)
    forcing = jnp.dot(couple.T, flux_share, precision=lax.Precision.HIGHEST)
    ocean_new = ocean_state + mask_f[None, :] * jnp.tanh(forcing)
    sea_table = lax.all_gather(
        jnp.concatenate([mask_f[None, :] * ocean_new, mask_f[None, :]], axis=0),
        "ocn",
        axis=1,
        tiled=True,
    )
    picked = sea_table[:, remap_cell]
    sea_part = jnp.sum(remap_weight[None, :, :] * picked[:nsrf_count], axis=1)
    sea_share = jnp.sum(remap_weight * picked[nsrf_count], axis=0)
    level_count = feat_count // 2
    land_values = jnp.stack([new_state[:, level_count - 1], new_state[:, feat_count - 1]]).astype(
        jnp.float32
    )
    surface = sea_part + (1.0 - sea_share)[None, :] * land_values
    return (new_state, span_tend, ocean_new, surface)


def solution(mesh):
    return jax.shard_map(
        body,
        mesh=mesh,
        in_specs=(
            P(("atm", "ocn"), None),
            P(("atm", "ocn")),
            P(("atm", "ocn")),
            P(),
            P(),
            P(),
            P(),
            P(),
            P(None, ("atm", "ocn")),
            P(None, ("atm", "ocn")),
            P(None, ("atm", "ocn")),
            P(("atm", "ocn")),
            P(),
        ),
        out_specs=(
            P(("atm", "ocn"), None),
            P(("atm", "ocn"), None),
            P(None, ("atm", "ocn")),
            P(None, ("atm", "ocn")),
        ),
        check_vma=False,
    )
```

profile of v0, /device:TPU:24, one launch (start us, length us, event | category | flops | bytes accessed | tf_op | source)
XLA Modules:
  0.0 463.1 jit_solution(4418286445871202986)
XLA Ops:
  7.2 1.4 compare_select_fusion.9
  10.1 1.4 scatter_custom_fusion
  11.6 1.9 gather_fusion
  14.2 11.3 %all-to-all-start = ((s32[32,1,8]{2,1,0:T(1,128)}), s32[32,1,8]{2,1,0:T(1,128)S(1)}, u32[]{:S(2)}, u32[]{:S(2)}) async-start(s32[32,1,8]{2,1,0:T(1,128)} %bitcast.14), calls=%async_computation | async-start | bytes 32768 | tf_op jit(solution)/shard_map/all_to_all | solution.py:92
  27.8 7.4 %all-to-all-done = s32[32,1,8]{2,1,0:T(1,128)S(1)} async-done(((s32[32,1,8]{2,1,0:T(1,128)}), s32[32,1,8]{2,1,0:T(1,128)S(1)}, u32[]{:S(2)}, u32[]{:S(2)}) %all-to-all-start) | async-done | bytes 1056 | tf_op jit(solution)/shard_map/all_to_all | solution.py:92
  35.3 3.8 all-to-all-start.2
  39.1 1.5 concatenate.51
  40.6 3.7 gather_fusion.1
  44.3 4.5 all-to-all-done.2
  48.8 5.4 %all-to-all-start.1 = ((bf16[32,128,256]{2,1,0:T(8,128)(2,1)}), bf16[32,128,256]{2,1,0:T(8,128)(2,1)}, u32[]{:S(2)}, u32[]{:S(2)}) async-start(bf16[32,128,256]{2,1,0:T(8,128)(2,1)} %bitcast.134), calls=%async_computation.1 | async-start | bytes 4194304 | tf_op jit(solution)/shard_map/all_to_all | solution.py:95
  54.2 2.3 copy.53
  58.6 1.8 scatter_custom_fusion.2
  61.1 29.0 %scatter_custom_fusion.3 = s32[1024]{0:T(1024)S(1)} fusion(s32[4096]{0:T(1024)S(1)} %bitcast.152, s32[4096]{0:T(1024)S(1)} %broadcast.231, s32[]{:T(128)} %copy.80), kind=kCustom, calls=%fused_computation.95 | custom fusion | flops 4096 | bytes 4100 | tf_op jit(solution)/shard_map/scatter-add | solution.py:115
  92.0 10.9 %all-to-all-done.1 = bf16[32,128,256]{2,1,0:T(8,128)(2,1)} async-done(((bf16[32,128,256]{2,1,0:T(8,128)(2,1)}), bf16[32,128,256]{2,1,0:T(8,128)(2,1)}, u32[]{:S(2)}, u32[]{:S(2)}) %all-to-all-start.1) | async-done | bytes 2097184 | tf_op jit(solution)/shard_map/all_to_all | solution.py:95
  103.0 3.9 pad_maximum_fusion
  107.0 35.3 %scatter_fusion = bf16[256,16,256]{2,1,0:T(8,128)(2,1)S(1)} fusion(bf16[256,16,256]{2,1,0:T(8,128)(2,1)S(1)} %broadcast_in_dim.84, s32[512]{0:T(512)S(1)} %bitcast.156, bf16[512,16,256]{2,1,0:T(8,128)(2,1)} %pad_maximum_fusion), kind=kCustom, calls=%fused_computation.9 | custom fusion | bytes 12584960 | tf_op jit(solution)/shard_map/scatter | solution.py:100
  142.3 5.0 %gather_fusion.3 = bf16[1024,256]{1,0:T(8,128)(2,1)} fusion(bf16[4096,256]{1,0:T(8,128)(2,1)S(1)} %bitcast.126, s32[1024]{0:T(1024)S(1)} %broadcast_clamp_fusion.1), kind=kCustom, calls=%fused_computation.3 | custom fusion | bytes 1052672 | tf_op jit(solution)/shard_map/gather | solution.py:119
  147.3 6.0 %while.21 = (s32[]{:T(128)}, f32[2,512,256]{2,1,0:T(8,128)S(1)}, bf16[2,512,256]{2,1,0:T(8,128)(2,1)}, bf16[256,2048]{1,0:T(8,128)(2,1)}, bf16[2048,256]{1,0:T(8,128)(2,1)}, /*index=5*/s32[]{:T(128)}) while((s32[]{:T(128)}, f32[2,512,256]{2,1,0:T(8,128)S(1)}, bf16[2,512,256]{2,1,0:T(8,128)(2,1)}, bf16[256,2048]{1,0:T(8,128)(2,1)}, ...), condition=%wide.region_16.17_spmd, body=%wide.region_15.16_spmd.sunk | while | flops 1078984704 | bytes 2884677 | solution.py:34
  147.3 3.0 fusion.61
  150.3 3.0 fusion.61
  153.3 22.9 %while.20 = (s32[]{:T(128)}, f32[8,512,256]{2,1,0:T(8,128)}, bf16[8,512,256]{2,1,0:T(8,128)(2,1)S(1)}, bf16[256,2048]{0,1:T(8,128)(2,1)}, s32[]{:T(128)}) while((s32[]{:T(128)}, f32[8,512,256]{2,1,0:T(8,128)}, bf16[8,512,256]{2,1,0:T(8,128)(2,1)S(1)}, bf16[256,2048]{0,1:T(8,128)(2,1)}, s32[]{:T(128)}) %tuple.56), condition=%wide.region_7.8_spmd, body=%wide.region_5.7_spmd.sunk | while | flops 537919488 | bytes 2884161 | solution.py:18
  153.3 2.0 tanh_reduce_fusion.2
  156.2 2.0 tanh_reduce_fusion.2
  159.0 2.0 tanh_reduce_fusion.2
  161.9 2.0 tanh_reduce_fusion.2
  164.8 2.0 tanh_reduce_fusion.2
  167.7 2.0 tanh_reduce_fusion.2
  170.5 2.0 tanh_reduce_fusion.2
  173.4 2.0 tanh_reduce_fusion.2
  176.2 10.1 %scatter_fusion.1 = f32[4096,256]{1,0:T(8,128)} fusion(f32[4096,256]{1,0:T(8,128)} %bitcast.128, s32[1024]{0:T(1024)S(1)} %bitcast.149, f32[1024,256]{1,0:T(8,128)S(1)} %bitcast.136), kind=kCustom, calls=%fused_computation.12 | custom fusion | flops 262144 | bytes 3149824 | tf_op jit(solution)/shard_map/scatter-add | solution.py:120
  186.3 2.4 convert_element_type.53
  188.8 1.3 copy-done.4
  190.2 2.1 gather_fusion.5
  192.4 6.7 %all-to-all-start.3 = ((bf16[32,128,256]{2,1,0:T(8,128)(2,1)}), bf16[32,128,256]{2,1,0:T(8,128)(2,1)}, u32[]{:S(2)}, u32[]{:S(2)}) async-start(bf16[32,128,256]{2,1,0:T(8,128)(2,1)} %bitcast.135), calls=%async_computation.3 | async-start | bytes 4194304 | tf_op jit(solution)/shard_map/all_to_all | solution.py:127
  199.8 2.6 fusion.34
  202.4 3.7 gather_fusion.4
  206.1 41.3 %all-to-all-done.3 = bf16[32,128,256]{2,1,0:T(8,128)(2,1)} async-done(((bf16[32,128,256]{2,1,0:T(8,128)(2,1)}), bf16[32,128,256]{2,1,0:T(8,128)(2,1)}, u32[]{:S(2)}, u32[]{:S(2)}) %all-to-all-start.3) | async-done | bytes 2097184 | tf_op jit(solution)/shard_map/all_to_all | solution.py:127
  247.4 3.7 gather_fusion.6
  251.1 5.0 %fusion.14 = (bf16[4096,256]{1,0:T(8,128)(2,1)}, bf16[4096,256]{1,0:T(8,128)(2,1)S(1)}) fusion(f32[256,256,16]{1,2,0:T(8,128)} %fusion.34, bf16[4096,256]{1,0:T(8,128)(2,1)S(1)} %copy-done.2, bf16[256,16,256]{2,1,0:T(8,128)(2,1)} %gather_fusion.6, bf16[256,16,256]{2,1,0:T(8,128)(2,1)} %gather_fusion.4, pred[4096]{0:T(1024)(128)(4,1)S(1)} %broadcast_in_dim.81), kind=kLoop, calls=%fused_computation.30 | loop fusion | flops 6291456 | bytes 14684160 | tf_op jit(solution)/shard_map/convert_element_type | solution.py:136
  257.1 5.1 %copy.55 = f32[16384,4]{1,0:T(8,128)} copy(f32[16384,4]{0,1:T(4,128)S(1)} %broadcast_multiply_fusion) | data formatting | bytes 524288 | tf_op jit(solution)/shard_map/mul | solution.py:143
  262.2 88.1 %scatter_custom_fusion.5 = f32[4096,4]{1,0:T(8,128)S(1)} fusion(s32[16384]{0:T(1024)S(1)} %bitcast.146, f32[16384,4]{1,0:T(8,128)} %copy.55, f32[]{:T(128)} %constant.127.clone.1), kind=kCustom, calls=%fused_computation.39 | custom fusion | flops 65536 | bytes 66048 | tf_op jit(solution)/shard_map/scatter-add | solution.py:144
  350.3 1.1 convert_bitcast_fusion
  351.4 2.9 slice_reduce_fusion.1
  354.4 25.7 %reduce-scatter.2.cloned.1.call-done = bf16[4,512]{0,1:T(8,128)(2,1)} async-done(((bf16[4,4096]{0,1:T(8,128)(2,1)}), bf16[4,512]{0,1:T(8,128)(2,1)}) %reduce-scatter.2.cloned.1.call-update) | async-done | bytes 4112 | tf_op jit(solution)/shard_map/reduce_scatter | solution.py:145
  380.1 1.7 broadcast_multiply_fusion.1
  381.8 13.2 %all_gather.3 = f32[3,4096]{1,0:T(4,128)S(1)} all-gather(f32[3,512]{1,0:T(4,128)S(1)} %pad_maximum_fusion.1), channel_id=1, replica_groups=mesh['atm'=32,'ocn'=8] {'ocn'}, dimensions={1}, use_global_device_ids=true | all-gather | bytes 55296 | tf_op jit(solution)/shard_map/all_gather | solution.py:150
  395.7 54.4 %gather_fusion.7 = f32[16384,3]{1,0:T(8,128)} fusion(f32[3,4096]{0,1:T(8,128)S(1)} %copy.56, s32[16384]{0:T(1024)S(1)} %broadcast_clamp_fusion), kind=kCustom, calls=%fused_computation.7 | custom fusion | bytes 458752 | tf_op jit(solution)/shard_map/gather | solution.py:156
  450.1 5.3 %copy.57 = f32[4,4096,3]{1,0,2:T(4,128)S(1)} copy(f32[4,4096,3]{2,1,0:T(8,128)} %bitcast.132) | data formatting | bytes 393216 | tf_op jit(solution)/shard_map/gather | solution.py:156
  (107 shorter events, 19.3 us)
Async XLA Ops:
  7.2 192.6 %copy-start = (bf16[16,16]{1,0:T(8,128)(2,1)S(1)}, bf16[16,16]{1,0:T(8,128)(2,1)}, u32[]{:S(2)}) copy-start(bf16[16,16]{1,0:T(8,128)(2,1)} %param.20) | copy-start | bytes 1540
  7.2 31.9 %copy-start.1 = (bf16[4096,256]{1,0:T(8,128)(2,1)S(1)}, bf16[4096,256]{1,0:T(8,128)(2,1)}, u32[]{:S(2)}) copy-start(bf16[4096,256]{1,0:T(8,128)(2,1)} %param.17) | copy-start | bytes 6291460
  10.1 15.4 %copy-start.7 = (pred[256]{0:T(512)(128)(4,1)}, pred[256]{0:T(512)(128)(4,1)S(1)}, u32[]{:S(2)}) copy-start(pred[256]{0:T(512)(128)(4,1)S(1)} %get-tuple-element.104) | copy-start | bytes 772
  14.2 21.0 %all-to-all-start = ((s32[32,1,8]{2,1,0:T(1,128)}), s32[32,1,8]{2,1,0:T(1,128)S(1)}, u32[]{:S(2)}, u32[]{:S(2)}) async-start(s32[32,1,8]{2,1,0:T(1,128)} %bitcast.14), calls=%async_computation | async-start | bytes 32768 | tf_op jit(solution)/shard_map/all_to_all | solution.py:92
  35.3 13.6 %all-to-all-start.2 = ((s32[32,1,128]{2,1,0:T(1,128)}), s32[32,1,128]{2,1,0:T(1,128)S(1)}, u32[]{:S(2)}, u32[]{:S(2)}) async-start(s32[32,1,128]{2,1,0:T(1,128)} %bitcast.20), calls=%async_computation.2 | async-start | bytes 32768 | tf_op jit(solution)/shard_map/all_to_all | solution.py:93
  48.8 54.1 %all-to-all-start.1 = ((bf16[32,128,256]{2,1,0:T(8,128)(2,1)}), bf16[32,128,256]{2,1,0:T(8,128)(2,1)}, u32[]{:S(2)}, u32[]{:S(2)}) async-start(bf16[32,128,256]{2,1,0:T(8,128)(2,1)} %bitcast.134), calls=%async_computation.1 | async-start | bytes 4194304 | tf_op jit(solution)/shard_map/all_to_all | solution.py:95
  188.7 1.3 copy-start.4
  190.2 2.1 copy-start.3
  192.3 7.1 %copy-start.8 = (pred[256]{0:T(512)(128)(4,1)S(1)}, pred[256]{0:T(512)(128)(4,1)}, u32[]{:S(2)}) copy-start(pred[256]{0:T(512)(128)(4,1)} %copy-done.7) | copy-start | bytes 772
  192.3 7.3 %copy-start.5 = (f32[4,4096]{1,0:T(4,128)S(1)}, f32[4,4096]{1,0:T(4,128)}, u32[]{:S(2)}) copy-start(f32[4,4096]{1,0:T(4,128)} %param.26) | copy-start | bytes 196612
  192.3 7.3 %copy-start.6 = (s32[4,4096]{1,0:T(4,128)S(1)}, s32[4,4096]{1,0:T(4,128)}, u32[]{:S(2)}) copy-start(s32[4,4096]{1,0:T(4,128)} %param.25) | copy-start | bytes 196612
  192.3 7.3 %copy-start.13 = (s32[512]{0:T(512)S(1)}, s32[512]{0:T(512)}, u32[]{:S(2)}) copy-start(s32[512]{0:T(512)} %param.28) | copy-start | bytes 6148
  192.3 7.4 %copy-start.11 = (s32[256]{0:T(256)S(1)}, s32[256]{0:T(256)}, u32[]{:S(2)}) copy-start(s32[256]{0:T(256)} %get-tuple-element.103) | copy-start | bytes 3076
  192.3 7.4 %copy-start.10 = (s32[256]{0:T(256)S(1)}, s32[256]{0:T(256)}, u32[]{:S(2)}) copy-start(s32[256]{0:T(256)} %get-tuple-element.101) | copy-start | bytes 3076
  192.3 7.4 %copy-start.2 = (bf16[4096,256]{1,0:T(8,128)(2,1)S(1)}, bf16[4096,256]{1,0:T(8,128)(2,1)}, u32[]{:S(2)}) copy-start(bf16[4096,256]{1,0:T(8,128)(2,1)} %param.17) | copy-start | bytes 6291460
  192.4 55.1 %all-to-all-start.3 = ((bf16[32,128,256]{2,1,0:T(8,128)(2,1)}), bf16[32,128,256]{2,1,0:T(8,128)(2,1)}, u32[]{:S(2)}, u32[]{:S(2)}) async-start(bf16[32,128,256]{2,1,0:T(8,128)(2,1)} %bitcast.135), calls=%async_computation.3 | async-start | bytes 4194304 | tf_op jit(solution)/shard_map/all_to_all | solution.py:127
  199.1 181.0 %reduce-scatter.2.cloned.1.call-start = ((), (), s32[]{:S(2)}) async-start(), calls=%async_computation.5 | async-start | bytes 1179648 | tf_op jit(solution)/shard_map/reduce_scatter | solution.py:145
  251.1 5.0 %copy-start.12 = (bf16[256,4]{0,1:T(4,128)(2,1)S(1)}, bf16[256,4]{0,1:T(4,128)(2,1)}, u32[]{:S(2)}) copy-start(bf16[256,4]{0,1:T(4,128)(2,1)} %param.24) | copy-start | bytes 6148
  351.4 28.7 %copy-start.9 = (f32[2,512]{1,0:T(2,128)S(1)}, f32[2,512]{1,0:T(2,128)}, u32[]{:S(2)}) copy-start(f32[2,512]{1,0:T(2,128)} %param.27) | copy-start | bytes 12292
  351.4 28.7 %copy-start.14 = (f32[4,2]{0,1:T(2,128)S(1)}, f32[4,2]{0,1:T(2,128)}, u32[]{:S(2)}) copy-start(f32[4,2]{0,1:T(2,128)} %param.29) | copy-start | bytes 100
Sparse Core Ops, SparseCore 0:
  351.5 28.5 reduce-scatter.1
where the time goes:
time: 469 us; the launch traced here: 463 us
  other arithmetic  155 us (33%)
  local copies, waits for them, and re-layouts  135 us (29%)
  waiting for transfers between devices  89.9 us (19%)
  starting transfers between devices  27.5 us (6%)
  matrix products  27.1 us (6%)
  between operations  14.6 us (3%)
  blocking collectives  13.2 us (3%)
    scatter-add x1, other arithmetic, body(): jax.ops.segment_sum(weighted, remap_cell.reshape(-1), num_segments=oc_grp)  88.1 us
    gather x2, local copies, waits for them, and re-layouts, body(): picked = sea_table[:, remap_cell]  59.7 us
    all_to_all x1, waiting for transfers between devices, body(): lax.all_to_all(send_back, 'atm', split_axis=0, concat_axis=0, tiled=True)  41.3 us
    scatter x1, local copies, waits for them, and re-layouts, body(): span_cols = jnp.zeros((elem_count, node_count, feat_count), jnp.bfloat16)...  35.3 us
    scatter-add x1, other arithmetic, body(): jnp.nonzero(span_branch.reshape(col_count) == 1, size=col_count // 4)[0]  29 us
    reduce_scatter x1, waiting for transfers between devices, body(): lax.psum_scatter(flux_term.astype(jnp.bfloat16), 'ocn', scatter_dimension...  25.7 us
    dot_general x8, matrix products, radiation_one_block(): jnp.dot(rows_in, rad_weight, preferred_element_type=jnp.float32)  16.1 us
    all_gather x1, blocking collectives, body(): lax.all_gather(jnp.concatenate([mask_f[None, :] * ocean_new, mask_f[None,...  13.2 us
  transfers between devices with their start and end apart: 5, of which 5 were waited for; matrix products, arithmetic and copies ran while one was open for 12% of the time, Pallas kernels for 0%

commit v1 on v0

v1 whole, which is shorter than its diff:
```python
import jax
import jax.numpy as jnp
from jax import lax
from jax.experimental import pallas as pl
from jax.experimental.pallas import tpu as pltpu
from jax.sharding import PartitionSpec as P

MESH = pl.DeviceIdType.MESH
F32 = jnp.float32
BF16 = jnp.bfloat16
I32 = jnp.int32

NX, NZ = 4, 8
NPEER = NX * NZ - 1
NOCN = 8
NE = 256
ND = 16
NF = 256
ROWS = NE * ND
MOVE = 8
MROWS = MOVE * ND
NMOVED = NE // 2
RB = 256
EB = RB // ND
NB = ROWS // RB
NBM = NMOVED // EB
CB = 512
PLACE = 32


def iota(shape, dim):
    return lax.broadcasted_iota(I32, shape, dim)


def onehot(cond):
    return jnp.where(cond, 1.0, 0.0).astype(F32)


def dot(a, b):
    return jnp.dot(a, b, preferred_element_type=F32)


def dot_nt(a, b):
    return lax.dot_general(a, b, (((1,), (1,)), ((), ())), preferred_element_type=F32)


def column(row):
    parts = [
        jnp.broadcast_to(row[:, h * 128 : (h + 1) * 128], (128, 128)).T for h in range(2)
    ]
    half = jnp.concatenate(parts, axis=0)
    return jnp.concatenate([half, half], axis=1)


def plan_kernel(
    span_hbm, branch_hbm, deriv_hbm, scal, msg_out, mask_ord, dblk, span_ref, branch_ref, deriv_ref, sem
):
    copies = [
        pltpu.make_async_copy(src, dst, sem.at[n])
        for n, (src, dst) in enumerate(
            [(span_hbm, span_ref), (branch_hbm, branch_ref), (deriv_hbm, deriv_ref)]
        )
    ]
    for copy in copies:
        copy.start()
    atm = lax.axis_index("atm")
    x = atm // NZ
    z = lax.rem(atm, NZ)
    for copy in copies:
        copy.wait()
    span = span_ref[...]
    slot_r = (span & (NE - 1)).astype(F32)
    target = span >> 11
    rel = ((((target >> 3) - x) & (NX - 1)) << 3) + (((target & (NZ - 1)) - z) & (NZ - 1))
    key_i = jnp.where(rel == 0, NPEER, rel - 1)
    key_r = key_i.astype(F32)
    both_r = (key_i * NE + iota((1, NE), 1)).astype(F32)
    key_c = column(key_r)
    both_c = column(both_r)
    lane = iota((NE, NE), 1).astype(F32)
    sub = iota((NE, NE), 0).astype(F32)
    pos_r = jnp.sum(onehot(both_c < both_r), axis=0, keepdims=True)
    less_r = jnp.sum(onehot(key_c < key_r), axis=0, keepdims=True)
    base_r = jnp.sum(onehot(key_c < lane), axis=0, keepdims=True)
    pos_c = column(pos_r)
    src_r = jnp.sum(jnp.where(pos_c == lane, sub, 0.0), axis=0, keepdims=True)
    scal[0:1, :] = src_r.astype(I32)
    scal[1:2, :] = pos_r.astype(I32)
    scal[2:3, :] = base_r.astype(I32)
    rank_r = jnp.where(key_r == NPEER, pos_r - (NMOVED - 1), pos_r - less_r + 1.0)
    pick = jnp.where(key_r == iota((32, NE), 0).astype(F32), rank_r, 0.0).astype(BF16)
    slots = onehot(column(slot_r) == lane).astype(BF16)
    msg = dot(pick, slots)
    packed = (msg[:, :128] + 256.0 * msg[:, 128:]).astype(I32)
    for i in range(32):
        msg_out[i] = packed[i : i + 1, :]
    bits = branch_ref[...].astype(F32).astype(BF16)
    spread = dot(onehot(iota((NE, 32), 0) // 8 == iota((NE, 32), 1)).astype(BF16), bits)
    own = jnp.where(iota((NE, 128), 1) // ND == iota((NE, 128), 0) % 8, spread, 0.0)
    fold = onehot(iota((128, 128), 0) % ND == iota((128, 128), 1) % ND).astype(BF16)
    bits_nat = dot(own.astype(BF16), fold).astype(BF16)
    order = onehot(pos_r == sub).astype(BF16)
    mask_ord[...] = dot(order, bits_nat).astype(BF16)
    spread_rows = onehot(iota((RB, ND), 0) % ND == iota((RB, ND), 1)).astype(BF16)
    tiled = dot_nt(dot(spread_rows, deriv_ref[...]).astype(BF16), spread_rows)
    same = iota((RB, RB), 0) // ND == iota((RB, RB), 1) // ND
    dblk[...] = jnp.where(same, tiled, 0.0).astype(BF16)


def kernel(
    scal,
    msg_out,
    mask_ord,
    dblk,
    couple_hbm,
    fw_hbm,
    cell_hbm,
    weight_hbm,
    ostate_hbm,
    omask_hbm,
    state_hbm,
    rad_hbm,
    cin_hbm,
    cout_hbm,
    new_ref,
    pool,
    q_v,
    onew_ref,
    surf_ref,
    state,
    rad,
    cin,
    cout,
    fw_ref,
    cell_ref,
    weight_ref,
    ostate_ref,
    omask_ref,
    couple_ref,
    xs,
    ordered,
    send,
    msg_in,
    scal_s,
    flux16,
    land,
    facc,
    rs_out,
    rs_in,
    table,
    load_sem,
    dsend,
    drecv,
    msend,
    mrecv,
    rsend,
    rrecv,
    asend,
    arecv,
):
    atm = lax.axis_index("atm")
    ocn = lax.axis_index("ocn")
    x = atm // NZ
    z = lax.rem(atm, NZ)

    def peer(i):
        rel = i + 1
        return lax.rem(x + rel // NZ, NX) * NZ + lax.rem(z + lax.rem(rel, NZ), NZ)

    def sea(q):
        return lax.rem(ocn + q, NOCN)

    barrier = pltpu.get_barrier_semaphore()
    loads = [
        pltpu.make_async_copy(src, dst, load_sem.at[n])
        for n, (src, dst) in enumerate(
            [
                (state_hbm, state),
                (rad_hbm, rad),
                (cin_hbm, cin),
                (cout_hbm, cout),
                (fw_hbm, fw_ref),
                (cell_hbm, cell_ref),
                (weight_hbm, weight_ref),
                (ostate_hbm, ostate_ref),
                (omask_hbm, omask_ref),
                (couple_hbm, couple_ref),
            ]
        )
    ]
    for copy in loads:
        copy.start()

    @pl.loop(0, NPEER)
    def _(i):
        pl.semaphore_signal(barrier, inc=1, device_id=(peer(i), ocn), device_id_type=MESH)

    @pl.loop(1, NOCN)
    def _(q):
        pl.semaphore_signal(barrier, inc=1, device_id=(atm, sea(q)), device_id_type=MESH)

    scal_copy = pltpu.make_async_copy(scal, scal_s, load_sem.at[10])
    scal_copy.start()
    for copy in loads:
        copy.wait()
    scal_copy.wait()

    to_rows = onehot(iota((RB, EB), 0) // ND == iota((RB, EB), 1)).astype(BF16)
    my_lane = iota((RB, 128), 1) == iota((RB, 128), 0) % ND
    ones = jnp.ones((128, NF), BF16)

    def physics(b):
        for j in range(EB):
            at = scal_s[0, b * EB + j] * ND
            xs[j * ND : (j + 1) * ND, :] = state[pl.ds(at, ND), :]
        cols = xs[...]
        total = jnp.zeros((RB, NF), F32)
        conv = jnp.zeros((RB, NF), F32)
        for g in range(8):
            part = slice(g * NF, (g + 1) * NF)
            total += jnp.tanh(dot(cols, rad[:, part]))
            half = 0.5 * dot(cols, cin[:, part])
            hidden = (half * (1.0 + jnp.tanh(half))).astype(BF16)
            conv += dot(hidden, cout[part, :])
        bits_b = mask_ord[pl.ds(pl.multiple_of(b * EB, EB), EB), :]
        mine = jnp.where(my_lane, dot(to_rows, bits_b), 0.0).astype(BF16)
        mask = dot(mine, ones)
        out = (0.25 * total + mask * conv).astype(BF16)
        ordered[pl.ds(pl.multiple_of(b * RB, RB), RB), :] = out
        return out

    def data_copy(i):
        return pltpu.make_async_remote_copy(
            src_ref=send.at[i],
            dst_ref=pool.at[pl.ds(pl.multiple_of(i * MROWS, MROWS), MROWS)],
            send_sem=dsend.at[i],
            recv_sem=drecv.at[i],
            device_id=(peer(i), ocn),
            device_id_type=MESH,
        )

    def msg_copy(i):
        return pltpu.make_async_remote_copy(
            src_ref=msg_out.at[i],
            dst_ref=msg_in.at[i],
            send_sem=msend.at[i],
            recv_sem=mrecv.at[i],
            device_id=(peer(i), ocn),
            device_id_type=MESH,
        )

    def ship(i):
        at = scal_s[2, i] * ND
        send[i] = ordered[pl.ds(at, MROWS), :]
        msg_copy(i).start()
        data_copy(i).start()

    per_block = EB // MOVE
    physics(0)
    pl.semaphore_wait(barrier, NPEER + NOCN - 1)
    for i in range(per_block):
        ship(i)

    @pl.loop(1, NBM)
    def _(b):
        physics(b)
        for i in range(per_block):
            ship(b * per_block + i)

    @pl.loop(NBM * per_block, NPEER)
    def _(i):
        ship(i)

    @pl.loop(NBM, NB)
    def _(b):
        at = NPEER * MROWS + (b - NBM) * RB
        pool[pl.ds(pl.multiple_of(at, MROWS), RB), :] = physics(b)

    rep = onehot(iota((16, 4), 0) // 4 == iota((16, 4), 1)).astype(BF16)
    fw16 = dot(rep, fw_ref[...]).astype(BF16)
    level = jnp.where(iota((16, NF), 0) == 0, NF // 2 - 1, NF - 1)
    ends = onehot((iota((16, NF), 1) == level) & (iota((16, NF), 0) < 2)).astype(BF16)

    @pl.loop(0, NB)
    def _(b):
        for j in range(EB):
            at = scal_s[1, b * EB + j] * ND
            xs[j * ND : (j + 1) * ND, :] = ordered[pl.ds(at, ND), :]
        tend = xs[...]
        rows = pl.ds(pl.multiple_of(b * RB, RB), RB)
        old = state[rows, :]
        new = (old.astype(F32) + dot(dblk[...], old) + tend.astype(F32)).astype(BF16)
        new_ref[rows, :] = new
        flux16[:, rows] = dot_nt(fw16, tend)
        land[:, rows] = dot_nt(ends, new)

    row_hi = (iota((128, CB), 0) // 16) * 4 + iota((128, CB), 0) % 4
    row_lo = iota((128, CB), 0)
    facc[...] = jnp.zeros((128, 128), F32)

    @pl.loop(0, ROWS // CB)
    def _(c):
        cols = pl.ds(pl.multiple_of(c * CB, CB), CB)
        vals = flux16[:, cols]
        acc = jnp.zeros((128, 128), F32)
        for k in range(4):
            cell = cell_ref[k : k + 1, cols]
            weighted = vals * weight_ref[k : k + 1, cols]
            spread_w = jnp.concatenate([weighted] * 8, axis=0)
            a = jnp.where(row_hi == (cell >> 7), spread_w, 0.0).astype(BF16)
            b = onehot(row_lo == (cell & 127)).astype(BF16)
            acc += dot_nt(a, b)
        facc[...] += acc

    rs_out[...] = facc[...].astype(BF16)

    def rs_copy(q):
        return pltpu.make_async_remote_copy(
            src_ref=rs_out.at[pl.ds(pl.multiple_of(sea(q) * 16, 16), 16)],
            dst_ref=rs_in.at[q],
            send_sem=rsend.at[q],
            recv_sem=rrecv.at[q],
            device_id=(atm, sea(q)),
            device_id_type=MESH,
        )

    def ag_copy(q):
        return pltpu.make_async_remote_copy(
            src_ref=table.at[ocn],
            dst_ref=table.at[ocn],
            send_sem=asend.at[q],
            recv_sem=arecv.at[q],
            device_id=(atm, sea(q)),
            device_id_type=MESH,
        )

    for q in range(1, NOCN):
        rs_copy(q).start()
    share = facc[pl.ds(pl.multiple_of(ocn * 16, 16), 16), :]
    for q in range(1, NOCN):
        rs_copy(q).wait()
        share += rs_in[q].astype(F32)
    sea_mask = omask_ref[...].astype(F32)
    rows_out = []
    for s in range(2):
        forcing = jnp.zeros((4, 128), F32)
        for f in range(4):
            forcing += couple_ref[s, f] * share[f * 4 : (f + 1) * 4, :]
        old = jnp.concatenate(
            [ostate_ref[s : s + 1, h * 128 : (h + 1) * 128] for h in range(4)], axis=0
        )
        new = old + sea_mask * jnp.tanh(forcing)
        for h in range(4):
            onew_ref[s : s + 1, h * 128 : (h + 1) * 128] = new[h : h + 1, :]
        rows_out.append(sea_mask * new)
    table[ocn] = jnp.concatenate(rows_out + [sea_mask, jnp.zeros((4, 128), F32)], axis=0)
    for q in range(1, NOCN):
        ag_copy(q).start()

    def msg_wait(i, places):
        msg_copy(i).wait()
        got = msg_in[i]
        both = jnp.concatenate([got & 255, got >> 8], axis=0)
        return places + jnp.where(both > 0, both + (i * MOVE - 1), 0)

    got = msg_out[NPEER]
    both = jnp.concatenate([got & 255, got >> 8], axis=0)
    places = jnp.where(both > 0, both + (NPEER * MOVE - 1), 0)
    q_v[...] = lax.fori_loop(0, NPEER, msg_wait, places)
    for q in range(1, NOCN):
        ag_copy(q).wait()
    whole = table[...].reshape(128, 128)
    coarse = whole.astype(BF16)
    fine = (whole - coarse.astype(F32)).astype(BF16)
    split = jnp.concatenate([coarse, fine], axis=1)

    @pl.loop(0, ROWS // CB)
    def _(c):
        cols = pl.ds(pl.multiple_of(c * CB, CB), CB)
        acc = jnp.zeros((16, CB), F32)
        for k in range(4):
            cell = cell_ref[k : k + 1, cols]
            b = onehot(row_lo == (cell & 127)).astype(BF16)
            got = dot(split, jnp.concatenate([b, b], axis=0))
            got = jnp.where(row_hi == (cell >> 7), got, 0.0)
            part = got[0:16]
            for o in range(1, 8):
                part += got[o * 16 : (o + 1) * 16]
            acc += part * weight_ref[k : k + 1, cols]
        rest = 1.0 - jnp.sum(acc[8:12], axis=0, keepdims=True)
        ground = land[:, cols]
        for s in range(2):
            sea_part = jnp.sum(acc[s * 4 : (s + 1) * 4], axis=0, keepdims=True)
            surf_ref[s : s + 1, cols] = sea_part + rest * ground[s : s + 1]

    @pl.loop(0, NPEER)
    def _(i):
        data_copy(i).wait()


def place_kernel(q_hbm, pool, new_ref, onew_ref, surf_ref, new_out, tend_out, onew_out, surf_out, stage, q_s, sem):
    copies = [
        pltpu.make_async_copy(src, dst, sem.at[n])
        for n, (src, dst) in enumerate(
            [(q_hbm, q_s), (new_ref, new_out), (onew_ref, onew_out), (surf_ref, surf_out)]
        )
    ]
    for copy in copies:
        copy.start()
    copies[0].wait()

    def part(n):
        rows = pl.ds(pl.multiple_of(n * PLACE * ND, PLACE * ND), PLACE * ND)
        return pltpu.make_async_copy(stage.at[rows], tend_out.at[rows], sem.at[4 + n])

    @pl.loop(0, NE // PLACE)
    def _(n):
        for j in range(PLACE):
            s = n * PLACE + j
            at = pl.multiple_of(q_s[s // 128, lax.rem(s, 128)] * ND, ND)
            stage[pl.ds(pl.multiple_of(s * ND, ND), ND), :] = pool[pl.ds(at, ND), :]
        part(n).start()

    for copy in copies[1:]:
        copy.wait()

    @pl.loop(0, NE // PLACE)
    def _(n):
        part(n).wait()


def body(
    state,
    branch_id,
    span_map,
    derivative,
    rad_weight,
    conv_in,
    conv_out,
    flux_weight,
    remap_cell,
    remap_weight,
    ocean_state,
    ocean_mask,
    couple,
):
    vmem = pl.BlockSpec(memory_space=pltpu.VMEM)
    hbm = pl.BlockSpec(memory_space=pltpu.HBM)
    dma = pltpu.SemaphoreType.DMA
    in_hbm = lambda a: pltpu.with_memory_space_constraint(a, pltpu.HBM)
    stay = lambda a: pltpu.with_memory_space_constraint(a, pltpu.VMEM)
    in_vmem = pltpu.VMEM
    out_hbm = pltpu.HBM
    plan = pl.pallas_call(
        plan_kernel,
        out_shape=(
            in_vmem((8, NE), I32),
            in_vmem((32, 1, 128), I32),
            in_vmem((NE, 128), BF16),
            in_vmem((RB, RB), BF16),
        ),
        in_specs=[hbm] * 3,
        out_specs=(vmem,) * 4,
        scratch_shapes=[
            pltpu.VMEM((1, NE), I32),
            pltpu.VMEM((32, 128), I32),
            pltpu.VMEM((ND, ND), BF16),
            dma((3,)),
        ],
        compiler_params=pltpu.CompilerParams(vmem_limit_bytes=8 << 20),
    )(in_hbm(span_map.reshape(1, NE)), in_hbm(branch_id.reshape(32, 128)), in_hbm(derivative))
    new_state, pool, places, ocean_new, surface = pl.pallas_call(
        kernel,
        out_shape=(
            in_vmem((ROWS, NF), BF16),
            in_vmem((NPEER * MROWS + NMOVED * ND, NF), BF16),
            in_vmem((2, 128), I32),
            in_vmem((2, 512), F32),
            in_vmem((2, ROWS), F32),
        ),
        in_specs=[vmem] * 4 + [hbm] * 10,
        out_specs=(vmem,) * 5,
        scratch_shapes=[
            pltpu.VMEM((ROWS, NF), BF16),
            pltpu.VMEM((NF, 2048), BF16),
            pltpu.VMEM((NF, 2048), BF16),
            pltpu.VMEM((2048, NF), BF16),
            pltpu.VMEM((4, NF), BF16),
            pltpu.VMEM((4, ROWS), I32),
            pltpu.VMEM((4, ROWS), F32),
            pltpu.VMEM((2, 512), F32),
            pltpu.VMEM((4, 128), I32),
            pltpu.SMEM((2, 4), F32),
            pltpu.VMEM((RB, NF), BF16),
            pltpu.VMEM((ROWS, NF), BF16),
            pltpu.VMEM((NPEER, MROWS, NF), BF16),
            pltpu.VMEM((32, 1, 128), I32),
            pltpu.SMEM((8, NE), I32),
            pltpu.VMEM((16, ROWS), F32),
            pltpu.VMEM((16, ROWS), F32),
            pltpu.VMEM((128, 128), F32),
            pltpu.VMEM((128, 128), BF16),
            pltpu.VMEM((NOCN, 16, 128), BF16),
            pltpu.VMEM((NOCN, 16, 128), F32),
            dma((11,)),
            dma((NPEER,)),
            dma((NPEER,)),
            dma((NPEER,)),
            dma((NPEER,)),
            dma((NOCN,)),
            dma((NOCN,)),
            dma((NOCN,)),
            dma((NOCN,)),
        ],
        compiler_params=pltpu.CompilerParams(
            collective_id=0, has_side_effects=True, vmem_limit_bytes=32 << 20
        ),
        cost_estimate=pl.CostEstimate(
            flops=14_000_000_000, bytes_accessed=12_000_000, transcendentals=17_000_000
        ),
    )(
        *plan,
        *(
            in_hbm(a)
            for a in (
                couple.T,
                flux_weight.T,
                remap_cell,
                remap_weight,
                ocean_state,
                ocean_mask.reshape(4, 128),
                state,
                rad_weight,
                conv_in,
                conv_out,
            )
        ),
    )
    new_state, span_tend, ocean_new, surface = pl.pallas_call(
        place_kernel,
        out_shape=(
            out_hbm((ROWS, NF), BF16),
            out_hbm((ROWS, NF), BF16),
            out_hbm((2, 512), F32),
            out_hbm((2, ROWS), F32),
        ),
        in_specs=[vmem] * 5,
        out_specs=(hbm,) * 4,
        scratch_shapes=[
            pltpu.VMEM((ROWS, NF), BF16),
            pltpu.SMEM((2, 128), I32),
            dma((4 + NE // PLACE,)),
        ],
        compiler_params=pltpu.CompilerParams(vmem_limit_bytes=8 << 20),
    )(*(stay(a) for a in (places, pool, new_state, ocean_new, surface)))
    return new_state, span_tend, ocean_new, surface


def solution(mesh):
    cols = P(("atm", "ocn"), None)
    flat = P(("atm", "ocn"))
    lanes = P(None, ("atm", "ocn"))
    return jax.shard_map(
        body,
        mesh=mesh,
        in_specs=(cols, flat, flat, P(), P(), P(), P(), P(), lanes, lanes, lanes, flat, P()),
        out_specs=(cols, cols, lanes, lanes),
        check_vma=False,
    )
```

time: 469 us -> 68.8 us (0.15); the launches traced: 463 us -> 68.7 us
  other arithmetic: 155 us -> 0 us
  local copies, waits for them, and re-layouts: 135 us -> 0 us
  waiting for transfers between devices: 89.9 us -> 0 us
  Pallas kernels: 0 us -> 68 us
  starting transfers between devices: 27.5 us -> 0 us
  matrix products: 27.1 us -> 0 us
  between operations: 14.6 us -> 0.65 us
  blocking collectives: 13.2 us -> 0 us
    scatter-add x3 -> x0, other arithmetic: 127 us -> none  [the longest x1 88.1 us: body(): jax.ops.segment_sum(weighted, remap_cell.reshape(-1), num_segments=oc_grp)]
    gather x9 -> x0, local copies, waits for them, and re-layouts: 80.5 us -> none  [the longest x2 59.7 us: body(): picked = sea_table[:, remap_cell]]
    pallas_call x0 -> x3, Pallas kernels: none -> 68 us  [the longest x1 63.3 us: body(): pl.pallas_call(kernel, out_shape=(in_vmem((ROWS, NF), BF16), in_vmem((NPE...]
    all_to_all x4 -> x0, waiting for transfers between devices: 64.2 us -> none  [the longest x1 41.3 us: body(): lax.all_to_all(send_back, 'atm', split_axis=0, concat_axis=0, tiled=True)]
    scatter x2 -> x0, local copies, waits for them, and re-layouts: 36.7 us -> none  [the longest x1 35.3 us: body(): span_cols = jnp.zeros((elem_count, node_count, feat_count), jnp.bfloat16)...]
    all_to_all x4 -> x0, starting transfers between devices: 27.3 us -> none  [the longest x1 11.3 us: body(): lax.all_to_all(send_slot, 'atm', split_axis=0, concat_axis=0, tiled=True)]
    dot_general x13 -> x0, matrix products: 27.1 us -> none  [the longest x8 16.1 us: radiation_one_block(): jnp.dot(rows_in, rad_weight, preferred_element_type=jnp.float32)]
    reduce_scatter x1 -> x0, waiting for transfers between devices: 25.7 us -> none  [body(): lax.psum_scatter(flux_term.astype(jnp.bfloat16), 'ocn', scatter_dimension...]
  transfers between devices with their start and end apart: 5 -> 0, of which waited for: 5 -> 0; matrix products, arithmetic and copies ran while one was open for 12% -> 0% of each run, Pallas kernels for 0% -> 0%
where the time goes in v1:
time: 68.8 us; the launch traced here: 68.7 us
  Pallas kernels  68 us (99%)
    pallas_call x1, Pallas kernels, body(): pl.pallas_call(kernel, out_shape=(in_vmem((ROWS, NF), BF16), in_vmem((NPE...  63.3 us
    pallas_call x1, Pallas kernels, body(): pl.pallas_call(place_kernel, out_shape=(out_hbm((ROWS, NF), BF16), out_hb...  3.36 us

profile of v1, /device:TPU:24, one launch (start us, length us, event | category | flops | bytes accessed | tf_op | source)
XLA Modules:
  0.0 68.7 jit_solution(16388290611143207731)
XLA Ops:
  0.6 1.3 %shard_map.156 = (s32[8,256]{1,0:T(8,128)S(1)}, s32[32,1,128]{2,1,0:T(1,128)S(1)}, bf16[256,128]{1,0:T(8,128)(2,1)S(1)}, bf16[256,256]{1,0:T(8,128)(2,1)S(1)}) custom-call(s32[1,256]{1,0:T(1,128)} %bitcast.6, s32[32,128]{1,0:T(8,128)} %bitcast.5, bf16[16,16]{1,0:T(8,128)(2,1)} %deriv_hbm.1), custom_call_target="tpu_custom_call" | custom-call | tf_op jit(solution)/shard_map/pallas_call | solution.py:454
  2.0 63.3 %shard_map.157 = (bf16[4096,256]{1,0:T(8,128)(2,1)S(1)}, bf16[6016,256]{1,0:T(8,128)(2,1)S(1)}, s32[2,128]{1,0:T(2,128)S(1)}, f32[2,512]{1,0:T(2,128)S(1)}, f32[2,4096]{1,0:T(2,128)S(1)}) custom-call(s32[8,256]{1,0:T(8,128)S(1)} %get-tuple-element.13.scal, s32[32,1,128]{2,1,0:T(1,128)S(1)} %get-tuple-element.14.msg_out, ...), custom_call_target="tpu_custom_call" | custom-call | flops 14000000000 | bytes 12000000 | tf_op jit(solution)/shard_map/pallas_call | solution.py:472
  65.3 3.4 %shard_map.158 = (bf16[4096,256]{1,0:T(8,128)(2,1)}, bf16[4096,256]{1,0:T(8,128)(2,1)}, f32[2,512]{1,0:T(2,128)}, f32[2,4096]{1,0:T(2,128)}) custom-call(s32[2,128]{1,0:T(2,128)S(1)} %get-tuple-element.17.q_hbm, bf16[6016,256]{1,0:T(8,128)(2,1)S(1)} %get-tuple-element.18.pool, bf16[4096,256]{1,0:T(8,128)(2,1)S(1)} %get-tuple-element.19.new_ref, ...), custom_call_target="tpu_custom_call" | custom-call | tf_op jit(solution)/shard_map/pallas_call | solution.py:539

commit v2 on v1

--- a/solution.py
+++ b/solution.py
@@ -13,6 +13,7 @@
 NX, NZ = 4, 8
 NPEER = NX * NZ - 1
 NOCN = 8
+NY = 4
 NE = 256
 ND = 16
 NF = 256
@@ -25,7 +26,7 @@
 NB = ROWS // RB
 NBM = NMOVED // EB
 CB = 512
-PLACE = 32
+PLACE = 16
 
 
 def iota(shape, dim):
@@ -52,44 +53,136 @@
     return jnp.concatenate([half, half], axis=1)
 
 
-def plan_kernel(
-    span_hbm, branch_hbm, deriv_hbm, scal, msg_out, mask_ord, dblk, span_ref, branch_ref, deriv_ref, sem
+def kernel(
+    span_hbm,
+    branch_hbm,
+    deriv_hbm,
+    couple_hbm,
+    fw_hbm,
+    cell_hbm,
+    weight_hbm,
+    ostate_hbm,
+    omask_hbm,
+    state_hbm,
+    rad_hbm,
+    cin_hbm,
+    cout_hbm,
+    new_ref,
+    pool,
+    q_v,
+    onew_ref,
+    surf_ref,
+    span_ref,
+    branch_ref,
+    deriv_ref,
+    couple_ref,
+    fw_ref,
+    cell_ref,
+    weight_ref,
+    ostate_ref,
+    omask_ref,
+    state,
+    rad,
+    cin,
+    cout,
+    ordered,
+    mask_ord,
+    send,
+    msg_out,
+    msg_in,
+    scal_v,
+    scal_s,
+    dblk,
+    flux16,
+    land,
+    facc,
+    rs_out,
+    rs_in,
+    table,
+    second,
+    load_sem,
+    dsend,
+    drecv,
+    msend,
+    mrecv,
+    rsend,
+    rrecv,
+    asend,
+    arecv,
 ):
-    copies = [
-        pltpu.make_async_copy(src, dst, sem.at[n])
-        for n, (src, dst) in enumerate(
-            [(span_hbm, span_ref), (branch_hbm, branch_ref), (deriv_hbm, deriv_ref)]
-        )
-    ]
-    for copy in copies:
-        copy.start()
     atm = lax.axis_index("atm")
+    ocn = lax.axis_index("ocn")
     x = atm // NZ
     z = lax.rem(atm, NZ)
-    for copy in copies:
+    y = ocn // 2
+    core = lax.rem(ocn, 2)
+
+    def at_offset(dx, dz):
+        return lax.rem(x + dx, NX) * NZ + lax.rem(z + dz, NZ)
+
+    def peer(i):
+        rel = i + 1
+        return at_offset(rel // NZ, lax.rem(rel, NZ))
+
+    def sea(q):
+        return lax.rem(ocn + q, NOCN)
+
+    barrier = pltpu.get_barrier_semaphore()
+    along_x = [at_offset(dx, 0) for dx in range(1, NX)]
+    along_z = [at_offset(0, dz) for dz in range(1, NZ)]
+    along_y = [lax.rem(y + dy, NY) * 2 + core for dy in range(1, NY)]
+    mate = y * 2 + 1 - core
+    for to in along_z + along_x:
+        pl.semaphore_signal(barrier, inc=1, device_id=(to, ocn), device_id_type=MESH)
+    for to in along_y + [mate]:
+        pl.semaphore_signal(barrier, inc=1, device_id=(atm, to), device_id_type=MESH)
+    first_count = len(along_x) + len(along_z) + len(along_y) + 1
+
+    small = [(span_hbm, span_ref), (branch_hbm, branch_ref), (deriv_hbm, deriv_ref)]
+    large = [
+        (state_hbm, state),
+        (rad_hbm, rad),
+        (cin_hbm, cin),
+        (cout_hbm, cout),
+        (fw_hbm, fw_ref),
+        (cell_hbm, cell_ref),
+        (weight_hbm, weight_ref),
+        (ostate_hbm, ostate_ref),
+        (omask_hbm, omask_ref),
+        (couple_hbm, couple_ref),
+    ]
+    loads = [
+        pltpu.make_async_copy(src, dst, load_sem.at[n])
+        for n, (src, dst) in enumerate(small + large)
+    ]
+    for copy in loads:
+        copy.start()
+    for copy in loads[: len(small)]:
         copy.wait()
+
     span = span_ref[...]
-    slot_r = (span & (NE - 1)).astype(F32)
     target = span >> 11
     rel = ((((target >> 3) - x) & (NX - 1)) << 3) + (((target & (NZ - 1)) - z) & (NZ - 1))
-    key_i = jnp.where(rel == 0, NPEER, rel - 1)
-    key_r = key_i.astype(F32)
-    both_r = (key_i * NE + iota((1, NE), 1)).astype(F32)
+    key_r = jnp.where(rel == 0, NPEER, rel - 1)
+    both_r = key_r * NE + iota((1, NE), 1)
     key_c = column(key_r)
     both_c = column(both_r)
-    lane = iota((NE, NE), 1).astype(F32)
-    sub = iota((NE, NE), 0).astype(F32)
-    pos_r = jnp.sum(onehot(both_c < both_r), axis=0, keepdims=True)
-    less_r = jnp.sum(onehot(key_c < key_r), axis=0, keepdims=True)
-    base_r = jnp.sum(onehot(key_c < lane), axis=0, keepdims=True)
-    pos_c = column(pos_r)
-    src_r = jnp.sum(jnp.where(pos_c == lane, sub, 0.0), axis=0, keepdims=True)
-    scal[0:1, :] = src_r.astype(I32)
-    scal[1:2, :] = pos_r.astype(I32)
-    scal[2:3, :] = base_r.astype(I32)
-    rank_r = jnp.where(key_r == NPEER, pos_r - (NMOVED - 1), pos_r - less_r + 1.0)
-    pick = jnp.where(key_r == iota((32, NE), 0).astype(F32), rank_r, 0.0).astype(BF16)
-    slots = onehot(column(slot_r) == lane).astype(BF16)
+    lane = iota((NE, NE), 1)
+    sub = iota((NE, NE), 0)
+
+    def count(cond):
+        return jnp.sum(jnp.where(cond, 1, 0), axis=0, keepdims=True)
+
+    pos_r = count(both_c < both_r)
+    src_r = jnp.sum(jnp.where(column(pos_r) == lane, sub, 0), axis=0, keepdims=True)
+    scal_v[0:1, :] = src_r
+    scal_v[1:2, :] = pos_r
+    scal_v[2:3, :] = jnp.minimum(count(key_c < lane), NMOVED)
+    scal_copy = pltpu.make_async_copy(scal_v, scal_s, load_sem.at[len(loads)])
+    scal_copy.start()
+    rank_r = jnp.where(key_r == NPEER, pos_r - (NMOVED - 1), pos_r - count(key_c < key_r) + 1)
+    pick = jnp.where(key_r == iota((32, NE), 0), rank_r, 0).astype(F32).astype(BF16)
+    slots = onehot(column(span & (NE - 1)) == lane).astype(BF16)
     msg = dot(pick, slots)
     packed = (msg[:, :128] + 256.0 * msg[:, 128:]).astype(I32)
     for i in range(32):
@@ -105,103 +198,7 @@
     tiled = dot_nt(dot(spread_rows, deriv_ref[...]).astype(BF16), spread_rows)
     same = iota((RB, RB), 0) // ND == iota((RB, RB), 1) // ND
     dblk[...] = jnp.where(same, tiled, 0.0).astype(BF16)
-
-
-def kernel(
-    scal,
-    msg_out,
-    mask_ord,
-    dblk,
-    couple_hbm,
-    fw_hbm,
-    cell_hbm,
-    weight_hbm,
-    ostate_hbm,
-    omask_hbm,
-    state_hbm,
-    rad_hbm,
-    cin_hbm,
-    cout_hbm,
-    new_ref,
-    pool,
-    q_v,
-    onew_ref,
-    surf_ref,
-    state,
-    rad,
-    cin,
-    cout,
-    fw_ref,
-    cell_ref,
-    weight_ref,
-    ostate_ref,
-    omask_ref,
-    couple_ref,
-    xs,
-    ordered,
-    send,
-    msg_in,
-    scal_s,
-    flux16,
-    land,
-    facc,
-    rs_out,
-    rs_in,
-    table,
-    load_sem,
-    dsend,
-    drecv,
-    msend,
-    mrecv,
-    rsend,
-    rrecv,
-    asend,
-    arecv,
-):
-    atm = lax.axis_index("atm")
-    ocn = lax.axis_index("ocn")
-    x = atm // NZ
-    z = lax.rem(atm, NZ)
-
-    def peer(i):
-        rel = i + 1
-        return lax.rem(x + rel // NZ, NX) * NZ + lax.rem(z + lax.rem(rel, NZ), NZ)
-
-    def sea(q):
-        return lax.rem(ocn + q, NOCN)
-
-    barrier = pltpu.get_barrier_semaphore()
-    loads = [
-        pltpu.make_async_copy(src, dst, load_sem.at[n])
-        for n, (src, dst) in enumerate(
-            [
-                (state_hbm, state),
-                (rad_hbm, rad),
-                (cin_hbm, cin),
-                (cout_hbm, cout),
-                (fw_hbm, fw_ref),
-                (cell_hbm, cell_ref),
-                (weight_hbm, weight_ref),
-                (ostate_hbm, ostate_ref),
-                (omask_hbm, omask_ref),
-                (couple_hbm, couple_ref),
-            ]
-        )
-    ]
-    for copy in loads:
-        copy.start()
-
-    @pl.loop(0, NPEER)
-    def _(i):
-        pl.semaphore_signal(barrier, inc=1, device_id=(peer(i), ocn), device_id_type=MESH)
-
-    @pl.loop(1, NOCN)
-    def _(q):
-        pl.semaphore_signal(barrier, inc=1, device_id=(atm, sea(q)), device_id_type=MESH)
-
-    scal_copy = pltpu.make_async_copy(scal, scal_s, load_sem.at[10])
-    scal_copy.start()
-    for copy in loads:
+    for copy in loads[len(small) :]:
         copy.wait()
     scal_copy.wait()
 
@@ -209,11 +206,12 @@
     my_lane = iota((RB, 128), 1) == iota((RB, 128), 0) % ND
     ones = jnp.ones((128, NF), BF16)
 
+    def gather(ref, row, b):
+        rows = [ref[pl.ds(scal_s[row, b * EB + j] * ND, ND), :] for j in range(EB)]
+        return jnp.concatenate(rows, axis=0)
+
     def physics(b):
-        for j in range(EB):
-            at = scal_s[0, b * EB + j] * ND
-            xs[j * ND : (j + 1) * ND, :] = state[pl.ds(at, ND), :]
-        cols = xs[...]
+        cols = gather(state, 0, b)
         total = jnp.zeros((RB, NF), F32)
         conv = jnp.zeros((RB, NF), F32)
         for g in range(8):
@@ -227,7 +225,6 @@
         mask = dot(mine, ones)
         out = (0.25 * total + mask * conv).astype(BF16)
         ordered[pl.ds(pl.multiple_of(b * RB, RB), RB), :] = out
-        return out
 
     def data_copy(i):
         return pltpu.make_async_remote_copy(
@@ -252,29 +249,44 @@
     def ship(i):
         at = scal_s[2, i] * ND
         send[i] = ordered[pl.ds(at, MROWS), :]
-        msg_copy(i).start()
         data_copy(i).start()
 
     per_block = EB // MOVE
-    physics(0)
-    pl.semaphore_wait(barrier, NPEER + NOCN - 1)
-    for i in range(per_block):
-        ship(i)
-
-    @pl.loop(1, NBM)
+
+    @pl.loop(0, NB)
     def _(b):
         physics(b)
-        for i in range(per_block):
-            ship(b * per_block + i)
-
-    @pl.loop(NBM * per_block, NPEER)
-    def _(i):
-        ship(i)
-
-    @pl.loop(NBM, NB)
-    def _(b):
-        at = NPEER * MROWS + (b - NBM) * RB
-        pool[pl.ds(pl.multiple_of(at, MROWS), RB), :] = physics(b)
+
+        @pl.when(b == 0)
+        def _():
+            pl.semaphore_wait(barrier, first_count)
+            for to in along_x:
+                pl.semaphore_signal(second, inc=1, device_id=(to, ocn), device_id_type=MESH)
+            pl.semaphore_signal(second, inc=1, device_id=(atm, mate), device_id_type=MESH)
+
+        @pl.when(b == 3)
+        def _():
+            pl.semaphore_wait(second, len(along_x) + 1)
+
+            @pl.loop(0, NPEER)
+            def _(i):
+                msg_copy(i).start()
+
+        @pl.when(b < NBM)
+        def _():
+            for i in range(per_block):
+                ship(b * per_block + i)
+
+        @pl.when(b == NBM - 1)
+        def _():
+            @pl.loop(NBM * per_block, NPEER)
+            def _(i):
+                ship(i)
+
+    @pl.loop(0, NB - NBM)
+    def _(n):
+        at = pl.ds(pl.multiple_of(NPEER * MROWS + n * RB, MROWS), RB)
+        pool[at, :] = ordered[pl.ds(pl.multiple_of((NBM + n) * RB, RB), RB), :]
 
     rep = onehot(iota((16, 4), 0) // 4 == iota((16, 4), 1)).astype(BF16)
     fw16 = dot(rep, fw_ref[...]).astype(BF16)
@@ -283,10 +295,7 @@
 
     @pl.loop(0, NB)
     def _(b):
-        for j in range(EB):
-            at = scal_s[1, b * EB + j] * ND
-            xs[j * ND : (j + 1) * ND, :] = ordered[pl.ds(at, ND), :]
-        tend = xs[...]
+        tend = gather(ordered, 1, b)
         rows = pl.ds(pl.multiple_of(b * RB, RB), RB)
         old = state[rows, :]
         new = (old.astype(F32) + dot(dblk[...], old) + tend.astype(F32)).astype(BF16)
@@ -415,10 +424,13 @@
 
     @pl.loop(0, NE // PLACE)
     def _(n):
+        rows = []
         for j in range(PLACE):
             s = n * PLACE + j
             at = pl.multiple_of(q_s[s // 128, lax.rem(s, 128)] * ND, ND)
-            stage[pl.ds(pl.multiple_of(s * ND, ND), ND), :] = pool[pl.ds(at, ND), :]
+            rows.append(pool[pl.ds(at, ND), :])
+        block = pl.ds(pl.multiple_of(n * PLACE * ND, PLACE * ND), PLACE * ND)
+        stage[block, :] = jnp.concatenate(rows, axis=0)
         part(n).start()
 
     for copy in copies[1:]:
@@ -451,24 +463,6 @@
     stay = lambda a: pltpu.with_memory_space_constraint(a, pltpu.VMEM)
     in_vmem = pltpu.VMEM
     out_hbm = pltpu.HBM
-    plan = pl.pallas_call(
-        plan_kernel,
-        out_shape=(
-            in_vmem((8, NE), I32),
-            in_vmem((32, 1, 128), I32),
-            in_vmem((NE, 128), BF16),
-            in_vmem((RB, RB), BF16),
-        ),
-        in_specs=[hbm] * 3,
-        out_specs=(vmem,) * 4,
-        scratch_shapes=[
-            pltpu.VMEM((1, NE), I32),
-            pltpu.VMEM((32, 128), I32),
-            pltpu.VMEM((ND, ND), BF16),
-            dma((3,)),
-        ],
-        compiler_params=pltpu.CompilerParams(vmem_limit_bytes=8 << 20),
-    )(in_hbm(span_map.reshape(1, NE)), in_hbm(branch_id.reshape(32, 128)), in_hbm(derivative))
     new_state, pool, places, ocean_new, surface = pl.pallas_call(
         kernel,
         out_shape=(
@@ -478,31 +472,38 @@
             in_vmem((2, 512), F32),
             in_vmem((2, ROWS), F32),
         ),
-        in_specs=[vmem] * 4 + [hbm] * 10,
+        in_specs=[hbm] * 13,
         out_specs=(vmem,) * 5,
         scratch_shapes=[
-            pltpu.VMEM((ROWS, NF), BF16),
-            pltpu.VMEM((NF, 2048), BF16),
-            pltpu.VMEM((NF, 2048), BF16),
-            pltpu.VMEM((2048, NF), BF16),
+            pltpu.VMEM((1, NE), I32),
+            pltpu.VMEM((32, 128), I32),
+            pltpu.VMEM((ND, ND), BF16),
+            pltpu.SMEM((2, 4), F32),
             pltpu.VMEM((4, NF), BF16),
             pltpu.VMEM((4, ROWS), I32),
             pltpu.VMEM((4, ROWS), F32),
             pltpu.VMEM((2, 512), F32),
             pltpu.VMEM((4, 128), I32),
-            pltpu.SMEM((2, 4), F32),
-            pltpu.VMEM((RB, NF), BF16),
             pltpu.VMEM((ROWS, NF), BF16),
+            pltpu.VMEM((NF, 2048), BF16),
+            pltpu.VMEM((NF, 2048), BF16),
+            pltpu.VMEM((2048, NF), BF16),
+            pltpu.VMEM((ROWS, NF), BF16),
+            pltpu.VMEM((NE, 128), BF16),
             pltpu.VMEM((NPEER, MROWS, NF), BF16),
             pltpu.VMEM((32, 1, 128), I32),
+            pltpu.VMEM((32, 1, 128), I32),
+            pltpu.VMEM((8, NE), I32),
             pltpu.SMEM((8, NE), I32),
+            pltpu.VMEM((RB, RB), BF16),
             pltpu.VMEM((16, ROWS), F32),
             pltpu.VMEM((16, ROWS), F32),
             pltpu.VMEM((128, 128), F32),
             pltpu.VMEM((128, 128), BF16),
             pltpu.VMEM((NOCN, 16, 128), BF16),
             pltpu.VMEM((NOCN, 16, 128), F32),
-            dma((11,)),
+            pltpu.SemaphoreType.REGULAR,
+            dma((14,)),
             dma((NPEER,)),
             dma((NPEER,)),
             dma((NPEER,)),
@@ -519,10 +520,12 @@
             flops=14_000_000_000, bytes_accessed=12_000_000, transcendentals=17_000_000
         ),
     )(
-        *plan,
         *(
             in_hbm(a)
             for a in (
+                span_map.reshape(1, NE),
+                branch_id.reshape(32, 128),
+                derivative,
                 couple.T,
                 flux_weight.T,
                 remap_cell,

time: 68.8 us -> 63.5 us (0.923)
  Pallas kernels: 68 us -> 62.7 us
    pallas_call x1, Pallas kernels: 63.3 us -> 59.5 us  [body(): pl.pallas_call(kernel, out_shape=(in_vmem((ROWS, NF), BF16), in_vmem((NPE...]
    pallas_call x1 -> x0, Pallas kernels: 1.33 us -> none  [body(): pl.pallas_call(plan_kernel, out_shape=(in_vmem((8, NE), I32), in_vmem((32...]
where the time goes in v2:
time: 63.5 us; the launch traced here: 63.4 us
  Pallas kernels  62.7 us (99%)
  between operations  0.64 us (1%)
    pallas_call x1, Pallas kernels, body(): pl.pallas_call(kernel, out_shape=(in_vmem((ROWS, NF), BF16), in_vmem((NPE...  59.5 us
    pallas_call x1, Pallas kernels, body(): pl.pallas_call(place_kernel, out_shape=(out_hbm((ROWS, NF), BF16), out_hb...  3.19 us

profile of v2, /device:TPU:24, one launch (start us, length us, event | category | flops | bytes accessed | tf_op | source)
XLA Modules:
  0.0 63.4 jit_solution(553945519948518836)
XLA Ops:
  0.6 59.5 %shard_map.156 = (bf16[4096,256]{1,0:T(8,128)(2,1)S(1)}, bf16[6016,256]{1,0:T(8,128)(2,1)S(1)}, s32[2,128]{1,0:T(2,128)S(1)}, f32[2,512]{1,0:T(2,128)S(1)}, f32[2,4096]{1,0:T(2,128)S(1)}) custom-call(s32[1,256]{1,0:T(1,128)} %bitcast.8, s32[32,128]{1,0:T(8,128)} %bitcast.5, bf16[16,16]{1,0:T(8,128)(2,1)} %deriv_hbm.1, f32[2,4]{1,0:T(2,128)} %bitcast.9, ...), custom_call_target="tpu_custom_call" | custom-call | flops 14000000000 | bytes 12000000 | tf_op jit(solution)/shard_map/pallas_call | solution.py:466
  60.2 3.2 %shard_map.157 = (bf16[4096,256]{1,0:T(8,128)(2,1)}, bf16[4096,256]{1,0:T(8,128)(2,1)}, f32[2,512]{1,0:T(2,128)}, f32[2,4096]{1,0:T(2,128)}) custom-call(s32[2,128]{1,0:T(2,128)S(1)} %get-tuple-element.9.q_hbm, bf16[6016,256]{1,0:T(8,128)(2,1)S(1)} %get-tuple-element.10.pool, bf16[4096,256]{1,0:T(8,128)(2,1)S(1)} %get-tuple-element.11.new_ref, ...), custom_call_target="tpu_custom_call" | custom-call | tf_op jit(solution)/shard_map/pallas_call | solution.py:542

commit v3 on v2

--- a/solution.py
+++ b/solution.py
@@ -69,7 +69,7 @@
     cout_hbm,
     new_ref,
     pool,
-    q_v,
+    q_s,
     onew_ref,
     surf_ref,
     span_ref,
@@ -100,6 +100,7 @@
     rs_in,
     table,
     second,
+    q_v,
     load_sem,
     dsend,
     drecv,
@@ -376,6 +377,9 @@
     both = jnp.concatenate([got & 255, got >> 8], axis=0)
     places = jnp.where(both > 0, both + (NPEER * MOVE - 1), 0)
     q_v[...] = lax.fori_loop(0, NPEER, msg_wait, places)
+    q_copy = pltpu.make_async_copy(q_v, q_s, load_sem.at[len(loads) + 1])
+    q_copy.start()
+    q_copy.wait()
     for q in range(1, NOCN):
         ag_copy(q).wait()
     whole = table[...].reshape(128, 128)
@@ -407,17 +411,15 @@
         data_copy(i).wait()
 
 
-def place_kernel(q_hbm, pool, new_ref, onew_ref, surf_ref, new_out, tend_out, onew_out, surf_out, stage, q_s, sem):
+def place_kernel(q_s, pool, new_ref, onew_ref, surf_ref, new_out, tend_out, onew_out, surf_out, stage, sem):
     copies = [
         pltpu.make_async_copy(src, dst, sem.at[n])
         for n, (src, dst) in enumerate(
-            [(q_hbm, q_s), (new_ref, new_out), (onew_ref, onew_out), (surf_ref, surf_out)]
+            [(new_ref, new_out), (onew_ref, onew_out), (surf_ref, surf_out)]
         )
     ]
     for copy in copies:
         copy.start()
-    copies[0].wait()
-
     def part(n):
         rows = pl.ds(pl.multiple_of(n * PLACE * ND, PLACE * ND), PLACE * ND)
         return pltpu.make_async_copy(stage.at[rows], tend_out.at[rows], sem.at[4 + n])
@@ -433,7 +435,7 @@
         stage[block, :] = jnp.concatenate(rows, axis=0)
         part(n).start()
 
-    for copy in copies[1:]:
+    for copy in copies:
         copy.wait()
 
     @pl.loop(0, NE // PLACE)
@@ -458,6 +460,7 @@
 ):
     vmem = pl.BlockSpec(memory_space=pltpu.VMEM)
     hbm = pl.BlockSpec(memory_space=pltpu.HBM)
+    smem = pl.BlockSpec(memory_space=pltpu.SMEM)
     dma = pltpu.SemaphoreType.DMA
     in_hbm = lambda a: pltpu.with_memory_space_constraint(a, pltpu.HBM)
     stay = lambda a: pltpu.with_memory_space_constraint(a, pltpu.VMEM)
@@ -468,12 +471,12 @@
         out_shape=(
             in_vmem((ROWS, NF), BF16),
             in_vmem((NPEER * MROWS + NMOVED * ND, NF), BF16),
-            in_vmem((2, 128), I32),
+            pltpu.SMEM((2, 128), I32),
             in_vmem((2, 512), F32),
             in_vmem((2, ROWS), F32),
         ),
         in_specs=[hbm] * 13,
-        out_specs=(vmem,) * 5,
+        out_specs=(vmem, vmem, smem, vmem, vmem),
         scratch_shapes=[
             pltpu.VMEM((1, NE), I32),
             pltpu.VMEM((32, 128), I32),
@@ -503,7 +506,8 @@
             pltpu.VMEM((NOCN, 16, 128), BF16),
             pltpu.VMEM((NOCN, 16, 128), F32),
             pltpu.SemaphoreType.REGULAR,
-            dma((14,)),
+            pltpu.VMEM((2, 128), I32),
+            dma((15,)),
             dma((NPEER,)),
             dma((NPEER,)),
             dma((NPEER,)),
@@ -547,15 +551,17 @@
             out_hbm((2, 512), F32),
             out_hbm((2, ROWS), F32),
         ),
-        in_specs=[vmem] * 5,
+        in_specs=[smem] + [vmem] * 4,
         out_specs=(hbm,) * 4,
         scratch_shapes=[
             pltpu.VMEM((ROWS, NF), BF16),
-            pltpu.SMEM((2, 128), I32),
             dma((4 + NE // PLACE,)),
         ],
         compiler_params=pltpu.CompilerParams(vmem_limit_bytes=8 << 20),
-    )(*(stay(a) for a in (places, pool, new_state, ocean_new, surface)))
+    )(
+        pltpu.with_memory_space_constraint(places, pltpu.SMEM),
+        *(stay(a) for a in (pool, new_state, ocean_new, surface)),
+    )
     return new_state, span_tend, ocean_new, surface
 
 

time: 63.5 us -> 62.9 us (level)
  no operation moved by 1% of the time
where the time goes in v3:
time: 62.9 us; the launch traced here: 62.8 us
  Pallas kernels  62.2 us (99%)
  between operations  0.64 us (1%)
    pallas_call x1, Pallas kernels, body(): pl.pallas_call(kernel, out_shape=(in_vmem((ROWS, NF), BF16), in_vmem((NPE...  59.6 us
    pallas_call x1, Pallas kernels, body(): pl.pallas_call(place_kernel, out_shape=(out_hbm((ROWS, NF), BF16), out_hb...  2.64 us

profile of v3, /device:TPU:24, one launch (start us, length us, event | category | flops | bytes accessed | tf_op | source)
XLA Modules:
  0.0 62.8 jit_solution(12188105474174794999)
XLA Ops:
  0.6 59.6 %shard_map.156 = (bf16[4096,256]{1,0:T(8,128)(2,1)S(1)}, bf16[6016,256]{1,0:T(8,128)(2,1)S(1)}, s32[2,128]{1,0:T(2,128)S(4)}, f32[2,512]{1,0:T(2,128)S(1)}, f32[2,4096]{1,0:T(2,128)S(1)}) custom-call(s32[1,256]{1,0:T(1,128)} %bitcast.8, s32[32,128]{1,0:T(8,128)} %bitcast.5, bf16[16,16]{1,0:T(8,128)(2,1)} %deriv_hbm.1, f32[2,4]{1,0:T(2,128)} %bitcast.9, ...), custom_call_target="tpu_custom_call" | custom-call | flops 14000000000 | bytes 12000000 | tf_op jit(solution)/shard_map/pallas_call | solution.py:469
  60.2 2.6 %shard_map.157 = (bf16[4096,256]{1,0:T(8,128)(2,1)}, bf16[4096,256]{1,0:T(8,128)(2,1)}, f32[2,512]{1,0:T(2,128)}, f32[2,4096]{1,0:T(2,128)}) custom-call(s32[2,128]{1,0:T(2,128)S(4)} %get-tuple-element.9.q_s, bf16[6016,256]{1,0:T(8,128)(2,1)S(1)} %get-tuple-element.10.pool, bf16[4096,256]{1,0:T(8,128)(2,1)S(1)} %get-tuple-element.11.new_ref, ...), custom_call_target="tpu_custom_call" | custom-call | tf_op jit(solution)/shard_map/pallas_call | solution.py:546

commit v4 on v3

--- a/solution.py
+++ b/solution.py
@@ -261,9 +261,6 @@
         @pl.when(b == 0)
         def _():
             pl.semaphore_wait(barrier, first_count)
-            for to in along_x:
-                pl.semaphore_signal(second, inc=1, device_id=(to, ocn), device_id_type=MESH)
-            pl.semaphore_signal(second, inc=1, device_id=(atm, mate), device_id_type=MESH)
 
         @pl.when(b == 3)
         def _():
@@ -277,6 +274,12 @@
         def _():
             for i in range(per_block):
                 ship(b * per_block + i)
+
+        @pl.when(b == 0)
+        def _():
+            for to in along_x:
+                pl.semaphore_signal(second, inc=1, device_id=(to, ocn), device_id_type=MESH)
+            pl.semaphore_signal(second, inc=1, device_id=(atm, mate), device_id_type=MESH)
 
         @pl.when(b == NBM - 1)
         def _():

time: 62.9 us -> 62.8 us (level)
  no operation moved by 1% of the time
where the time goes in v4:
time: 62.8 us
  Pallas kernels  62.1 us (99%)
  between operations  0.64 us (1%)
    pallas_call x1, Pallas kernels, body(): pl.pallas_call(kernel, out_shape=(in_vmem((ROWS, NF), BF16), in_vmem((NPE...  59.5 us
    pallas_call x1, Pallas kernels, body(): pl.pallas_call(place_kernel, out_shape=(out_hbm((ROWS, NF), BF16), out_hb...  2.64 us

profile of v4, /device:TPU:24, one launch (start us, length us, event | category | flops | bytes accessed | tf_op | source)
XLA Modules:
  0.0 62.8 jit_solution(8077787508563746307)
XLA Ops:
  0.6 59.5 %shard_map.156 = (bf16[4096,256]{1,0:T(8,128)(2,1)S(1)}, bf16[6016,256]{1,0:T(8,128)(2,1)S(1)}, s32[2,128]{1,0:T(2,128)S(4)}, f32[2,512]{1,0:T(2,128)S(1)}, f32[2,4096]{1,0:T(2,128)S(1)}) custom-call(s32[1,256]{1,0:T(1,128)} %bitcast.8, s32[32,128]{1,0:T(8,128)} %bitcast.5, bf16[16,16]{1,0:T(8,128)(2,1)} %deriv_hbm.1, f32[2,4]{1,0:T(2,128)} %bitcast.9, ...), custom_call_target="tpu_custom_call" | custom-call | flops 14000000000 | bytes 12000000 | tf_op jit(solution)/shard_map/pallas_call | solution.py:472
  60.1 2.6 %shard_map.157 = (bf16[4096,256]{1,0:T(8,128)(2,1)}, bf16[4096,256]{1,0:T(8,128)(2,1)}, f32[2,512]{1,0:T(2,128)}, f32[2,4096]{1,0:T(2,128)}) custom-call(s32[2,128]{1,0:T(2,128)S(4)} %get-tuple-element.9.q_s, bf16[6016,256]{1,0:T(8,128)(2,1)S(1)} %get-tuple-element.10.pool, bf16[4096,256]{1,0:T(8,128)(2,1)S(1)} %get-tuple-element.11.new_ref, ...), custom_call_target="tpu_custom_call" | custom-call | tf_op jit(solution)/shard_map/pallas_call | solution.py:549

commit v5 on v3

--- a/solution.py
+++ b/solution.py
@@ -26,7 +26,7 @@
 NB = ROWS // RB
 NBM = NMOVED // EB
 CB = 512
-PLACE = 16
+PLACE = 32
 
 
 def iota(shape, dim):

time: 62.9 us -> 62.9 us (level)
  no operation moved by 1% of the time
where the time goes in v5:
time: 62.9 us; the launch traced here: 62.8 us
  Pallas kernels  62.1 us (99%)
  between operations  0.64 us (1%)
    pallas_call x1, Pallas kernels, body(): pl.pallas_call(kernel, out_shape=(in_vmem((ROWS, NF), BF16), in_vmem((NPE...  59.6 us
    pallas_call x1, Pallas kernels, body(): pl.pallas_call(place_kernel, out_shape=(out_hbm((ROWS, NF), BF16), out_hb...  2.56 us

profile of v5, /device:TPU:24, one launch (start us, length us, event | category | flops | bytes accessed | tf_op | source)
XLA Modules:
  0.0 62.8 jit_solution(7210368958475841108)
XLA Ops:
  0.6 59.6 %shard_map.156 = (bf16[4096,256]{1,0:T(8,128)(2,1)S(1)}, bf16[6016,256]{1,0:T(8,128)(2,1)S(1)}, s32[2,128]{1,0:T(2,128)S(4)}, f32[2,512]{1,0:T(2,128)S(1)}, f32[2,4096]{1,0:T(2,128)S(1)}) custom-call(s32[1,256]{1,0:T(1,128)} %bitcast.8, s32[32,128]{1,0:T(8,128)} %bitcast.5, bf16[16,16]{1,0:T(8,128)(2,1)} %deriv_hbm.1, f32[2,4]{1,0:T(2,128)} %bitcast.9, ...), custom_call_target="tpu_custom_call" | custom-call | flops 14000000000 | bytes 12000000 | tf_op jit(solution)/shard_map/pallas_call | solution.py:469
  60.2 2.6 %shard_map.157 = (bf16[4096,256]{1,0:T(8,128)(2,1)}, bf16[4096,256]{1,0:T(8,128)(2,1)}, f32[2,512]{1,0:T(2,128)}, f32[2,4096]{1,0:T(2,128)}) custom-call(s32[2,128]{1,0:T(2,128)S(4)} %get-tuple-element.9.q_s, bf16[6016,256]{1,0:T(8,128)(2,1)S(1)} %get-tuple-element.10.pool, bf16[4096,256]{1,0:T(8,128)(2,1)S(1)} %get-tuple-element.11.new_ref, ...), custom_call_target="tpu_custom_call" | custom-call | tf_op jit(solution)/shard_map/pallas_call | solution.py:546
